TPU v7x, 128 devices: a whole 4x4x4 slice. The times are simulated.
128 devices in a mesh: bucket: 4 (over x), dp: 32 (over y, z, core).
Axes of the slice: x: 4, y: 4, z: 4, core: 2. Of those that a mesh axis runs over, the one named last changes fastest.
Arguments:
- queries: bfloat16 [4, 32, 1024, 1024], P('bucket', 'dp'), may hold values from -10 to 10
- bucket_ids: int32 [4, 32, 1024], P('bucket', 'dp'), may hold values from 0 to 3, as said below
- raw_passages: bfloat16 [4, 32, 192, 1024], P('bucket', 'dp'), may hold values from -8 to 8
- counts: int32 [4, 32], P('bucket', 'dp'), may hold values from 1 to 192, 2048 in all within a row
- teacher: bfloat16 [4, 32, 1024, 2048], P('bucket', 'dp'), may hold values from -16 to 320
Outputs:
- grad_queries: bfloat16 [4, 32, 1024, 1024], P('bucket', 'dp')
- grad_passages: bfloat16 [4, 2048, 1024], P('bucket', 'dp')
- kl_rows: float32 [4, 32, 1024], P('bucket', 'dp')
Inputs may be any that keep to these rules, and one draw needn't show every extreme that they name: `bucket_ids`: each device holds exactly 256 queries of each language. The counts of one language sum to 2048, and in every language one device holds exactly 192.
All inputs are finite; a program needn't handle non-finite values.
Results may differ from a plain program's by a relative error of at most 0.0075.
Values may be sent and summed in bfloat16 or wider, within the bound.
No kernel may reach another device: no remote copies, remote signals or barrier semaphores. Data moves between devices by JAX's collectives and lax.ppermute only.
A program may use at most 128 MiB of HBM per device.

v0:
```python
import functools

import jax
import jax.numpy as jnp
from jax import lax
from jax.experimental import pallas as pl
from jax.experimental.pallas import tpu as pltpu
from jax.sharding import Mesh
from jax.sharding import PartitionSpec as P

student_scale = 0.1
languages = 4
holders = 32
capacity = 192
width = 1024
per_device = 1024
per_language = 256
passages_all = 2048
both = width + passages_all
group_chunks = 8
group_rows = 256
window = 272
extra = 128
chunk_rows = 32
chunk_count = 96
store_rows = 6144
mib = 1024 * 1024


def slots_of(ids, here):
    turned = lax.rem(ids - here + languages, languages)
    kinds = lax.broadcasted_iota(jnp.int32, (8, per_device), 0)
    hot = (turned == kinds).astype(jnp.float32)
    parts = per_device // 128
    stacked = jnp.concatenate([hot[:, i * 128 : (i + 1) * 128] for i in range(parts)], axis=0)
    earlier = lax.broadcasted_iota(jnp.int32, (128, 128), 0)
    later = lax.broadcasted_iota(jnp.int32, (128, 128), 1)
    upper = (earlier <= later).astype(jnp.float32).astype(jnp.bfloat16)
    sums = jnp.dot(stacked.astype(jnp.bfloat16), upper, preferred_element_type=jnp.float32)
    before = jnp.zeros((8, 1), jnp.float32)
    ranks = []
    for i in range(parts):
        segment = sums[i * 8 : (i + 1) * 8]
        ranks.append(segment + before)
        before = before + segment[:, 127:128]
    place = jnp.concatenate(ranks, axis=1) - 1.0 + kinds.astype(jnp.float32) * per_language
    return jnp.sum(hot * place, axis=0, keepdims=True).astype(jnp.int32)


vmem = pl.BlockSpec(memory_space=pltpu.VMEM)
smem = pl.BlockSpec(memory_space=pltpu.SMEM)
hbm = pl.BlockSpec(memory_space=pltpu.HBM)


def call(kernel, name, in_specs, outs, scratch, limit, flops, transcendentals=0):
    return pl.pallas_call(
        kernel,
        in_specs=in_specs,
        out_specs=[spec for spec, _, _ in outs],
        out_shape=[jax.ShapeDtypeStruct(shape, dtype) for _, shape, dtype in outs],
        scratch_shapes=scratch,
        compiler_params=pltpu.CompilerParams(vmem_limit_bytes=limit * mib),
        cost_estimate=pl.CostEstimate(
            flops=flops, bytes_accessed=8 * mib, transcendentals=transcendentals
        ),
        name=name,
    )


def sort_kernel(
    first, here, ids, slot_in, queries, teacher, out_a, out_b, slot,
    select, block, moved_a, moved_b, in_sem, out_sem,
):
    tile = 512
    tiles = both // tile

    def read(j):
        source = queries if j < width // tile else teacher
        column = j * tile if j < width // tile else j * tile - width
        return pltpu.make_async_copy(
            source.at[:, pl.ds(column, tile)], block.at[j], in_sem.at[j]
        )

    def written(j):
        columns = pl.ds(j * tile, tile)
        return [
            pltpu.make_async_copy(moved_a.at[j], out_a.at[:, columns], out_sem.at[2 * j]),
            pltpu.make_async_copy(moved_b.at[j], out_b.at[:, columns], out_sem.at[2 * j + 1]),
        ]

    for j in range(tiles):
        read(j).start()
    if first:
        slots = slots_of(ids[...], here[0])
        slot[...] = jnp.broadcast_to(slots, (8, per_device))
    else:
        slots = slot_in[0:1, :]
        slot[...] = jnp.zeros((8, 128), jnp.int32)
    rows = lax.broadcasted_iota(jnp.int32, (per_language, per_device), 0)
    for half, number in enumerate((1, 3) if first else (2, 0)):
        hit = rows + number * per_language == slots
        select[pl.ds(half * per_language, per_language), :] = hit.astype(jnp.float32).astype(
            jnp.bfloat16
        )
    for j in range(tiles):
        read(j).wait()
        moved = jnp.dot(select[...], block[j], preferred_element_type=jnp.float32)
        moved_a[j] = moved[:per_language].astype(jnp.bfloat16)
        moved_b[j] = moved[per_language:].astype(jnp.bfloat16)
        for copy in written(j):
            copy.start()
    for j in range(tiles):
        for copy in written(j):
            copy.wait()


def sort_rows(here, ids, slot, queries, teacher):
    first = slot is None
    tiles = both // 512
    moved = pltpu.VMEM((tiles, per_language, 512), jnp.bfloat16)
    out = (hbm, (per_language, both), jnp.bfloat16)
    return call(
        functools.partial(sort_kernel, first),
        "sort_first" if first else "sort_rest",
        [smem, vmem, vmem, hbm, hbm],
        [out, out, (vmem, (8, per_device) if first else (8, 128), jnp.int32)],
        [
            pltpu.VMEM((2 * per_language, per_device), jnp.bfloat16),
            pltpu.VMEM((tiles, per_device, 512), jnp.bfloat16),
            moved,
            moved,
            pltpu.SemaphoreType.DMA((tiles,)),
            pltpu.SemaphoreType.DMA((2 * tiles,)),
        ],
        60 if first else 28,
        4 * per_language * per_device * both,
    )(here, ids, ids if first else slot, queries, teacher)


def kl_parts(value):
    high = value.astype(jnp.bfloat16).astype(jnp.float32)
    middle = (value - high).astype(jnp.bfloat16).astype(jnp.float32)
    low = value - high - middle
    lane = lax.broadcasted_iota(jnp.int32, value.shape, 1)
    parts = jnp.where(
        lane == 0, high, jnp.where(lane == 1, middle, jnp.where(lane == 2, low, 0.0))
    )
    return parts.astype(jnp.bfloat16)


def row_pass(quarter, scores, block, weights, kl):
    for i in range(4):
        local = pl.ds(pl.multiple_of(quarter * 64 + i * 16, 16), 16)
        own = scores[local, :]
        taught = block[local, :].astype(jnp.float32)
        top = jnp.max(own, axis=1, keepdims=True)
        taught_top = jnp.max(taught, axis=1, keepdims=True)
        grown = jnp.exp(own - top)
        total = jnp.sum(grown, axis=1, keepdims=True)
        shifted = taught - taught_top
        taught_grown = jnp.exp(shifted)
        taught_total = jnp.sum(taught_grown, axis=1, keepdims=True)
        cross = jnp.sum(taught_grown * (shifted - (own - top)), axis=1, keepdims=True)
        diverge = cross / taught_total - jnp.log(taught_total) + jnp.log(total)
        weights[local, :] = (
            grown * (student_scale / total) - taught_grown * (student_scale / taught_total)
        ).astype(jnp.bfloat16)
        kl[local, :] = jnp.broadcast_to(diverge, (16, 128))


def score_quarter(queries, base, quarter, passages, scores):
    columns = pl.ds(pl.multiple_of(quarter * 512, 512), 512)
    scores[:, columns] = (
        lax.dot_general(
            queries[pl.ds(base, per_language), pl.ds(0, width)],
            passages[columns, :],
            (((1,), (1,)), ((), ())),
            preferred_element_type=jnp.float32,
        )
        * student_scale
    )


def teacher_kernel(in0, in1, in2, store, queries, taught_out, parts, sems):
    rows = 3 * per_language

    def saved(number):
        block = pl.ds(number * per_language, per_language)
        behind = pl.ds(rows + number * per_language, per_language)
        return [
            pltpu.make_async_copy(taught_out.at[block], store.at[block], sems.at[number]),
            pltpu.make_async_copy(
                queries.at[block], store.at[behind, pl.ds(0, width)], sems.at[3 + number]
            ),
            pltpu.make_async_copy(
                parts.at[block], store.at[behind, pl.ds(width, extra)], sems.at[6 + number]
            ),
        ]

    for number, block in enumerate((in0, in1, in2)):

        def rows_of(i, carry, number=number, block=block):
            for part in range(4):
                local = pl.ds(pl.multiple_of(i * 64 + part * 16, 16), 16)
                placed = pl.ds(
                    pl.multiple_of(number * per_language + i * 64 + part * 16, 16), 16
                )
                queries[placed, :] = block[local, pl.ds(0, width)]
                taught = block[local, pl.ds(width, passages_all)].astype(jnp.float32)
                shifted = taught - jnp.max(taught, axis=1, keepdims=True)
                grown = jnp.exp(shifted)
                total = jnp.sum(grown, axis=1, keepdims=True)
                cross = jnp.sum(grown * shifted, axis=1, keepdims=True)
                taught_out[placed, :] = (grown * (student_scale / total)).astype(jnp.bfloat16)
                entropy = jnp.broadcast_to(cross / total - jnp.log(total), (16, 128))
                parts[placed, :] = kl_parts(entropy)
            return carry

        lax.fori_loop(0, 4, rows_of, 0)
        for copy in saved(number):
            copy.start()
    for number in range(3):
        for copy in saved(number):
            copy.wait()


def teacher_rows(blocks):
    rows = 3 * per_language
    return call(
        teacher_kernel,
        "teacher_rows",
        [vmem] * 3,
        [
            (hbm, (store_rows, passages_all), jnp.bfloat16),
            (vmem, (rows, width), jnp.bfloat16),
        ],
        [
            pltpu.VMEM((rows, passages_all), jnp.bfloat16),
            pltpu.VMEM((rows, extra), jnp.bfloat16),
            pltpu.SemaphoreType.DMA((9,)),
        ],
        40,
        mib,
        2 * mib,
    )(*blocks)


def student_pass(base, quarter, scores, taught_ref, parts, weights, kl):
    for i in range(4):
        local = pl.ds(pl.multiple_of(quarter * 64 + i * 16, 16), 16)
        placed = pl.ds(pl.multiple_of(base + quarter * 64 + i * 16, 16), 16)
        own = scores[local, :]
        taught = taught_ref[placed, :].astype(jnp.float32)
        shifted = own - jnp.max(own, axis=1, keepdims=True)
        grown = jnp.exp(shifted)
        total = jnp.sum(grown, axis=1, keepdims=True)
        cross = jnp.sum(taught * shifted, axis=1, keepdims=True)
        entropy = jnp.sum(
            parts[placed, pl.ds(width, extra)].astype(jnp.float32), axis=1, keepdims=True
        )
        diverge = entropy + jnp.log(total) - cross * (1.0 / student_scale)
        weights[placed, :] = (grown * (student_scale / total) - taught).astype(jnp.bfloat16)
        kl[placed, :] = jnp.broadcast_to(diverge, (16, 128))


def grad_columns(rows, columns, weights, passages, out):
    out[:, columns] = jnp.dot(
        weights[rows, :],
        passages[pl.ds(0, passages_all), columns],
        preferred_element_type=jnp.float32,
    ).astype(jnp.bfloat16)


def first_kernel(
    chunk_list, target_of, raw, store,
    weights, passages, kl, grad, raw_v, queries, taught, scores, other_scores, raw_sem, in_sem,
):
    def raw_copy(k):
        rows = pl.ds(pl.multiple_of(chunk_list[chunk_count + k], chunk_rows), chunk_rows)
        return pltpu.make_async_copy(raw.at[chunk_list[k], rows], raw_v.at[k], raw_sem.at[k])

    groups = chunk_list[3 * chunk_count]

    def start_group(g, carry):
        for c in range(group_chunks):
            raw_copy(g * group_chunks + c).start()
        return carry

    lax.fori_loop(0, groups, start_group, 0)
    copies = [
        pltpu.make_async_copy(
            store.at[pl.ds(3 * per_language, 3 * per_language), pl.ds(0, width + extra)],
            queries,
            in_sem.at[0],
        ),
        pltpu.make_async_copy(store.at[pl.ds(0, 3 * per_language)], taught, in_sem.at[1]),
    ]
    for copy in copies:
        copy.start()
    passages[pl.ds(0, 16), :] = jnp.zeros((16, width), jnp.bfloat16)

    def place(g, carry):
        for c in range(group_chunks):
            raw_copy(g * group_chunks + c).wait()
        start = pl.multiple_of((chunk_list[2 * chunk_count + g * group_chunks] // 16) * 16, 16)
        target = lax.broadcasted_iota(jnp.int32, (window, group_rows), 0)
        hit = target == target_of[pl.ds(g, 1), :] - start
        chosen = hit.astype(jnp.float32).astype(jnp.bfloat16)
        chunks = raw_v[pl.ds(g * group_chunks, group_chunks)].reshape(group_rows, width)
        moved = jnp.dot(chosen, chunks, preferred_element_type=jnp.float32).astype(jnp.bfloat16)
        head = passages[pl.ds(start, 16), :]
        passages[pl.ds(start, 16), :] = head + moved[:16]
        passages[pl.ds(start + 16, window - 16), :] = moved[16:]
        return carry

    lax.fori_loop(0, groups, place, 0)
    for copy in copies:
        copy.wait()

    def score_only(quarter, carry):
        score_quarter(queries, 0, quarter, passages, scores)
        return carry

    lax.fori_loop(0, 4, score_only, 0)
    held, free = scores, other_scores
    middle = pl.ds(per_language, per_language)
    for number in range(3):
        base = number * per_language

        def together(quarter, carry, base=base, held=held, free=free, last=number == 2):
            if last:
                columns = pl.ds(pl.multiple_of(quarter * 256, 256), 256)
                grad_columns(middle, columns, weights, passages, grad)
            else:
                score_quarter(queries, base + per_language, quarter, passages, free)
            student_pass(base, quarter, held, taught, queries, weights, kl)
            return carry

        lax.fori_loop(0, 4, together, 0)
        held, free = free, held
    grad[:, pl.ds(width, extra)] = kl_parts(kl[middle, :])


def first_blocks(chunk_list, raw, store):
    rows = 3 * per_language
    scores = pltpu.VMEM((per_language, passages_all), jnp.float32)
    return call(
        first_kernel,
        "first_blocks",
        [smem, vmem, hbm, hbm],
        [
            (vmem, (rows, passages_all), jnp.bfloat16),
            (vmem, (passages_all + window, width), jnp.bfloat16),
            (vmem, (rows, 128), jnp.float32),
            (vmem, (per_language, width + extra), jnp.bfloat16),
        ],
        [
            pltpu.VMEM((chunk_count, chunk_rows, width), jnp.bfloat16),
            pltpu.VMEM((rows, width + extra), jnp.bfloat16),
            pltpu.VMEM((rows, passages_all), jnp.bfloat16),
            scores,
            scores,
            pltpu.SemaphoreType.DMA((chunk_count,)),
            pltpu.SemaphoreType.DMA((2,)),
        ],
        40,
        6 * 1024**3,
        2 * mib,
    )(*chunk_list, raw, store)


def chunks_of(counts):
    number = (counts + chunk_rows - 1) // chunk_rows
    upto = jnp.arange(holders)[None, :] < jnp.arange(holders)[:, None]
    offsets = jnp.sum(jnp.where(upto, counts[None, :], 0), axis=1)
    firsts = jnp.sum(jnp.where(upto, number[None, :], 0), axis=1)
    index = jnp.arange(chunk_count)[:, None]
    mine = (index >= firsts[None, :]) & (index < (firsts + number)[None, :])
    row = (index - firsts[None, :]) * chunk_rows

    def pick(values):
        return jnp.sum(jnp.where(mine, values, 0), axis=1)

    holder = pick(jnp.arange(holders)[None, :] + 0 * row)
    used = pick(jnp.minimum(counts[None, :] - row, chunk_rows))
    place = jnp.where(used > 0, pick(offsets[None, :] + row), passages_all)
    slots = jnp.arange(chunk_rows)[None, :]
    groups = (jnp.sum(number) + group_chunks - 1) // group_chunks
    targets = jnp.where(slots < used[:, None], place[:, None] + slots, -1)
    return (
        jnp.concatenate([holder, pick(row), place, groups[None]]).astype(jnp.int32),
        targets.astype(jnp.int32).reshape(chunk_count // group_chunks, group_rows),
    )


def last_kernel(
    core, passages, before, queries, block, weights, send, keep, kl,
    own, teacher, scores, total, in_sem,
):
    own_copy = pltpu.make_async_copy(block.at[:, pl.ds(0, width)], own, in_sem.at[0])
    teacher_copy = pltpu.make_async_copy(
        block.at[:, pl.ds(width, passages_all)], teacher, in_sem.at[1]
    )
    own_copy.start()
    teacher_copy.start()
    own_copy.wait()

    def score_only(quarter, carry):
        score_quarter(own, 0, quarter, passages, scores)
        return carry

    lax.fori_loop(0, 4, score_only, 0)
    teacher_copy.wait()
    contract = (((0,), (0,)), ((), ()))

    def together(quarter, carry):
        row_pass(quarter, scores, teacher, weights, kl)
        columns = pl.ds(pl.multiple_of(quarter * 512, 512), 512)
        total[columns, :] = lax.dot_general(
            before[:, columns],
            queries[...],
            contract,
            preferred_element_type=jnp.float32,
        )
        return carry

    lax.fori_loop(0, 4, together, 0)
    even = core[0] == 0

    def reduce(j, carry):
        columns = pl.ds(pl.multiple_of(j * 256, 256), 256)
        grad = lax.dot_general(
            weights[:, columns],
            own[...],
            contract,
            preferred_element_type=jnp.float32,
        )
        grad = (grad + total[columns, :]).astype(jnp.bfloat16)
        for part in range(2):
            upper = grad[part * 128 : part * 128 + 64]
            lower = grad[part * 128 + 64 : part * 128 + 128]
            rows = pl.ds(pl.multiple_of(j * 128 + part * 64, 64), 64)
            keep[rows, :] = jnp.where(even, upper, lower)
            send[rows, :] = jnp.where(even, lower, upper)
        return carry

    lax.fori_loop(0, passages_all // 256, reduce, 0)


def last_block(core, passages, weights, queries, block):
    half = (vmem, (passages_all // 2, width), jnp.bfloat16)
    return call(
        last_kernel,
        "last_block",
        [smem] + [vmem] * 3 + [hbm],
        [
            (vmem, (per_language, passages_all), jnp.bfloat16),
            half,
            half,
            (vmem, (per_language, 128), jnp.float32),
        ],
        [
            pltpu.VMEM((per_language, width), jnp.bfloat16),
            pltpu.VMEM((per_language, passages_all), jnp.bfloat16),
            pltpu.VMEM((per_language, passages_all), jnp.float32),
            pltpu.VMEM((passages_all, width), jnp.float32),
            pltpu.SemaphoreType.DMA((2,)),
        ],
        20,
        6 * 1024**3,
        mib,
    )(core, passages, weights, queries, block)


def query_kernel(places, passages, *refs):
    for number, place in enumerate(places):
        weights, kl = refs[2 * number], refs[2 * number + 1]
        out = refs[2 * len(places) + number]
        rows = pl.ds(place * per_language, per_language)

        def step(half, carry, rows=rows, weights=weights, out=out):
            columns = pl.ds(pl.multiple_of(half * 512, 512), 512)
            grad_columns(rows, columns, weights, passages, out)
            return carry

        lax.fori_loop(0, 2, step, 0)
        out[:, pl.ds(width, extra)] = kl_parts(kl[rows, :])


def query_grads(places, passages, *arrays):
    return call(
        functools.partial(query_kernel, places),
        "query_grads",
        [vmem] * (1 + len(arrays)),
        [(vmem, (per_language, width + extra), jnp.bfloat16)] * len(places),
        [],
        8,
        len(places) * 1024**3,
    )(passages, *arrays)


def pair_kernel(keep, other, out):
    def step(i, carry):
        rows = pl.ds(pl.multiple_of(i * 64, 64), 64)
        out[rows, :] = (
            keep[rows, :].astype(jnp.float32) + other[rows, :].astype(jnp.float32)
        ).astype(jnp.bfloat16)
        return carry

    lax.fori_loop(0, passages_all // 128, step, 0)


def pair_sum(keep, other):
    return call(
        pair_kernel, "pair_sum", [vmem] * 2, [(vmem, keep.shape, jnp.bfloat16)], [], 8, mib
    )(keep, other)[0]


def selection(slot, numbers, select):
    rows = lax.broadcasted_iota(jnp.int32, (per_language, per_device), 0)
    for half, number in enumerate(numbers):
        hit = rows + number * per_language == slot[0:1, :]
        select[half * per_language : (half + 1) * per_language, :] = hit.astype(
            jnp.float32
        ).astype(jnp.bfloat16)


def joined(select, blocks, columns):
    part = None
    for half, block in enumerate(blocks):
        term = lax.dot_general(
            select[half * per_language : (half + 1) * per_language, :],
            block[:, columns],
            (((0,), (0,)), ((), ())),
            preferred_element_type=jnp.float32,
        )
        part = term if part is None else part + term
    return part


def restore_first_kernel(slot, in0, in1, in3, out, select):
    selection(slot, (0, 1, 3), select)
    blocks = (in0, in1, in3)

    def step(j, carry):
        columns = pl.ds(pl.multiple_of(j * 256, 256), 256)
        out[:, columns] = joined(select, blocks, columns).astype(jnp.bfloat16)
        return carry

    lax.fori_loop(0, width // 256, step, 0)
    columns = pl.ds(width, extra)
    out[:, columns] = joined(select, blocks, columns).astype(jnp.bfloat16)


def restore_last_kernel(slot, begun, in2, grads_out, kl, select, grads, out_sem):
    selection(slot, (2,), select)

    def written(j):
        columns = pl.ds(pl.multiple_of(j * 256, 256), 256)
        return pltpu.make_async_copy(grads.at[j], grads_out.at[:, columns], out_sem.at[j])

    def step(j, carry):
        columns = pl.ds(pl.multiple_of(j * 256, 256), 256)
        added = joined(select, (in2,), columns) + begun[:, columns].astype(jnp.float32)
        grads[j] = added.astype(jnp.bfloat16)
        written(j).start()
        return carry

    lax.fori_loop(0, width // 256, step, 0)
    columns = pl.ds(width, extra)
    parts = joined(select, (in2,), columns) + begun[:, columns].astype(jnp.float32)
    column = jnp.sum(parts, axis=1, keepdims=True)
    kl[...] = jnp.transpose(jnp.broadcast_to(column, (per_device, 128)))[:1]
    for j in range(width // 256):
        written(j).wait()


def restore_first(slot, blocks):
    return call(
        restore_first_kernel,
        "restore_first",
        [vmem] * 4,
        [(vmem, (per_device, width + extra), jnp.bfloat16)],
        [pltpu.VMEM((3 * per_language, per_device), jnp.bfloat16)],
        12,
        15 * 1024**3,
    )(slot, *blocks)[0]


def restore_last(slot, begun, block):
    return call(
        restore_last_kernel,
        "restore_last",
        [vmem] * 3,
        [
            (hbm, (per_device, width), jnp.bfloat16),
            (vmem, (1, per_device), jnp.float32),
        ],
        [
            pltpu.VMEM((per_language, per_device), jnp.bfloat16),
            pltpu.VMEM((width // 256, per_device, 256), jnp.bfloat16),
            pltpu.SemaphoreType.DMA((width // 256,)),
        ],
        12,
        1024**3,
    )(slot, begun, block)


def sum_kernel(pieces, out, held, sems):
    copies = []
    for i in range(4):
        rows = pl.ds(16 * i, 16)
        copies.append(pltpu.make_async_copy(pieces.at[:, rows], held.at[:, rows], sems.at[i]))
        copies[-1].start()
    for i, copy in enumerate(copies):
        copy.wait()
        total = held[0, 16 * i : 16 * (i + 1), :].astype(jnp.float32)
        for j in range(1, pieces.shape[0]):
            total = total + held[j, 16 * i : 16 * (i + 1), :].astype(jnp.float32)
        out[16 * i : 16 * (i + 1), :] = total.astype(jnp.bfloat16)


def sum_pieces(pieces):
    return call(
        sum_kernel,
        "sum_pieces",
        [hbm],
        [(vmem, (64, width), jnp.bfloat16)],
        [pltpu.VMEM(pieces.shape, jnp.bfloat16), pltpu.SemaphoreType.DMA((4,))],
        8,
        mib,
    )(pieces)[0]


def shift(array, by):
    pairs = [(i, (i + by) % languages) for i in range(languages)]
    return lax.ppermute(array, "x", pairs)


def on_device(queries, bucket_ids, raw_passages, counts, teacher):
    group = ("y", "z", "c")
    here = lax.axis_index("x").astype(jnp.int32).reshape(1)
    core = lax.axis_index("c").astype(jnp.int32).reshape(1)
    all_raw = lax.all_gather(raw_passages[0], group, axis=0, tiled=True)
    ids = bucket_ids[0]
    out1, out3, slot = sort_rows(here, ids, None, queries[0, 0], teacher[0, 0])
    in1, in3 = shift(out1, 1), shift(out3, 3)
    out2, in0, _ = sort_rows(here, ids, slot, queries[0, 0], teacher[0, 0])
    held_counts, in0, out2 = lax.optimization_barrier((counts, in0, out2))
    holder_counts = lax.all_gather(held_counts[0], group, axis=0, tiled=True)
    chunk_list = chunks_of(holder_counts)
    out2, in1, in3, chunk_list = lax.optimization_barrier((out2, in1, in3, chunk_list))
    in2 = shift(out2, 2)
    store, moved = teacher_rows((in0, in1, in3))
    all_raw, store, moved = lax.optimization_barrier((all_raw, store, moved))
    weights, passages, kl, back1 = first_blocks(chunk_list, all_raw, store)
    last_weights, send, keep, last_kl = last_block(core, passages, weights, moved, in2)
    other = lax.ppermute(send, "c", [(0, 1), (1, 0)])
    (back3,) = query_grads((2,), passages, weights, kl)
    keep, back3 = lax.optimization_barrier((keep, back3))
    home1, home3 = shift(back1, -1), shift(back3, -3)
    paired = pair_sum(keep, other)
    spread = lax.all_to_all(
        paired.reshape(16, 64, width), ("y", "z"), split_axis=0, concat_axis=0, tiled=True
    )
    paired, weights, last_weights = lax.optimization_barrier((paired, weights, last_weights))
    back2, back0 = query_grads((0, 0), passages, last_weights, last_kl, weights, kl)
    home2 = shift(back2, -2)
    grad_passages = sum_pieces(spread)
    begun = restore_first(slot, (back0, home1, home3))
    grad_queries, kl_rows = restore_last(slot, begun, home2)
    return (grad_queries[None, None], grad_passages[None], kl_rows[None])


def solution(mesh):
    split = Mesh(mesh.devices.reshape(4, 4, 4, 2), ("x", "y", "z", "c"))
    group = ("y", "z", "c")
    in_specs = (
        P("x", group, None, None),
        P("x", group, None),
        P("x", group, None, None),
        P("x", group),
        P("x", group, None, None),
    )
    out_specs = (P("x", group, None, None), P("x", group, None), P("x", group, None))
    return jax.shard_map(
        on_device, mesh=split, in_specs=in_specs, out_specs=out_specs, check_vma=False
    )
```

profile of v0, /device:TPU:0, one launch (start us, length us, event | category | flops | bytes accessed | tf_op | source)
XLA Modules:
  0.0 156.3 jit_solution(16422951807067987095)
XLA Ops:
  7.2 0.0 all-gather.4.cloned.1.call-start
  7.2 0.7 all-gather.4.cloned.1.call-update
  7.9 0.0 copy-start.18
  7.9 7.8 %sort_first.1 = (bf16[256,3072]{1,0:T(8,128)(2,1)}, bf16[256,3072]{1,0:T(8,128)(2,1)}, s32[8,1024]{1,0:T(8,128)}) custom-call(s32[1]{0:T(128)} %bitcast.here, s32[1,1024]{1,0:T(1,128)} %bitcast.19, s32[1,1024]{1,0:T(1,128)} %bitcast.20, bf16[1024,1024]{1,0:T(8,128)(2,1)} %bitcast.17, bf16[1024,2048]{1,0:T(8,128)(2,1)} %bitcast.15), custom_call_target="tpu_custom_call" | custom-call | flops 3221225472 | bytes 8388608 | tf_op jit(solution)/shard_map/sort_first/pallas_call | solution.py:122
  15.7 1.6 %collective-permute-start = (bf16[256,3072]{1,0:T(8,128)(2,1)}, bf16[256,3072]{1,0:T(8,128)(2,1)S(1)}, u32[]{:S(2)}, u32[]{:S(2)}) collective-permute-start(bf16[256,3072]{1,0:T(8,128)(2,1)} %get-tuple-element.41), channel_id=1, source_target_pairs={{0,32},{32,64},{64,96},{96,0},{1,33},{33,65},{65,97},{97,1},{2,34}... | collective-permute-start | bytes 4718600 | tf_op jit(solution)/shard_map/ppermute | solution.py:637
  17.3 1.7 %collective-permute-start.1 = (bf16[256,3072]{1,0:T(8,128)(2,1)}, bf16[256,3072]{1,0:T(8,128)(2,1)S(1)}, u32[]{:S(2)}, u32[]{:S(2)}) collective-permute-start(bf16[256,3072]{1,0:T(8,128)(2,1)} %get-tuple-element.42), channel_id=1, source_target_pairs={{0,96},{32,0},{64,32},{96,64},{1,97},{33,1},{65,33},{97,65},{2,98}... | collective-permute-start | bytes 4718600 | tf_op jit(solution)/shard_map/ppermute | solution.py:637
  19.6 0.0 copy-done.18
  19.7 0.6 dynamic-slice
  20.2 0.7 bitcast_dynamic-update-slice_fusion
  20.9 18.4 %all-reduce = s32[32]{0:T(128)S(1)} all-reduce(s32[32]{0:T(128)S(1)} %bitcast_dynamic-update-slice_fusion), channel_id=2, replica_groups=mesh['x'=4,'y'=4,'z'=4,'c'=2] {'y','z','c'}, use_global_device_ids=true, to_apply=%add | all-reduce | flops 32 | bytes 256 | tf_op jit(solution)/shard_map/all_gather | solution.py:650
  39.3 0.6 fusion.1
  40.6 0.1 select_reduce_fusion.1
  40.8 0.1 add.58
  40.8 0.1 select_reduce_fusion.4
  40.9 0.1 lt.51
  41.0 0.1 reduce_sum.72
  41.1 0.1 lt.52
  41.2 0.1 lt.53
  41.3 0.1 add.60
  41.4 0.1 add.61
  41.5 0.0 copy-start.10
  41.5 2.2 %copy-done.10 = bf16[1,1,1024,2048]{3,2,1,0:T(8,128)(2,1)S(1)} copy-done((bf16[1,1,1024,2048]{3,2,1,0:T(8,128)(2,1)S(1)}, bf16[1,1,1024,2048]{3,2,1,0:T(8,128)(2,1)}, u32[]{:S(2)}) %copy-start.10) | copy-done | bytes 4194328
  43.6 1.6 %copy-done.11 = bf16[1,1,1024,1024]{3,2,1,0:T(8,128)(2,1)S(1)} copy-done((bf16[1,1,1024,1024]{3,2,1,0:T(8,128)(2,1)S(1)}, bf16[1,1,1024,1024]{3,2,1,0:T(8,128)(2,1)}, u32[]{:S(2)}) %copy-start.11) | copy-done | bytes 2097176
  45.2 0.8 copy-done.16
  46.0 6.4 %sort_rest.1 = (bf16[256,3072]{1,0:T(8,128)(2,1)S(1)}, bf16[256,3072]{1,0:T(8,128)(2,1)S(1)}, s32[8,128]{1,0:T(8,128)}) custom-call(s32[1]{0:T(128)} %bitcast.here, s32[1,1024]{1,0:T(1,128)S(1)} %bitcast.21, s32[8,1024]{1,0:T(8,128)S(1)} %copy-done.16, bf16[1024,1024]{1,0:T(8,128)(2,1)S(1)} %bitcast.18, bf16[1024,2048]{1,0:T(8,128)(2,1)S(1)} %bitcast.16), custom_call_target="tpu_custom_call" | custom-call | flops 3221225472 | bytes 8388608 | tf_op jit(solution)/shard_map/sort_rest/pallas_call | solution.py:122
  52.4 0.0 copy-start.3
  52.4 1.1 copy-done.3
  53.6 1.1 copy-done.12
  54.7 0.7 pad_add_fusion.chunk_list
  55.3 0.0 collective-permute-done.in1
  55.3 0.0 collective-permute-done.1.in2
  55.4 1.8 %collective-permute-start.2 = (bf16[256,3072]{1,0:T(8,128)(2,1)}, bf16[256,3072]{1,0:T(8,128)(2,1)}, u32[]{:S(2)}, u32[]{:S(2)}) collective-permute-start(bf16[256,3072]{1,0:T(8,128)(2,1)} %copy-done.12), channel_id=1, source_target_pairs={{0,64},{32,96},{64,0},{96,32},{1,65},{33,97},{65,1},{97,33},{2,66}... | collective-permute-start | bytes 4718600 | tf_op jit(solution)/shard_map/ppermute | solution.py:637
  57.1 1.5 copy-done.4
  58.7 4.8 %teacher_rows.1 = (bf16[6144,2048]{1,0:T(8,128)(2,1)}, bf16[768,1024]{1,0:T(8,128)(2,1)S(1)}) custom-call(bf16[256,3072]{1,0:T(8,128)(2,1)S(1)} %copy-done.4, bf16[256,3072]{1,0:T(8,128)(2,1)S(1)} %collective-permute-done.in1, bf16[256,3072]{1,0:T(8,128)(2,1)S(1)} %collective-permute-done.1.in2), custom_call_target="tpu_custom_call" | custom-call | flops 1048576 | bytes 8388608 | tf_op jit(solution)/shard_map/teacher_rows/pallas_call | solution.py:229
  63.5 0.0 copy-start.13
  63.5 1.1 copy-done.13
  64.7 11.1 %all-gather.4.cloned.1.call-done = bf16[32,1,192,1024]{3,2,1,0:T(8,128)(2,1)} async-done(((bf16[1,1,192,1024]{3,2,1,0:T(8,128)(2,1)}), bf16[32,1,192,1024]{3,2,1,0:T(8,128)(2,1)}) %all-gather.4.cloned.1.call-update) | async-done | bytes 12582928 | tf_op jit(solution)/shard_map/all_gather | solution.py:644
  75.7 0.7 copy-done.9
  76.4 14.6 %first_blocks.1 = (bf16[768,2048]{1,0:T(8,128)(2,1)S(1)}, bf16[2320,1024]{1,0:T(8,128)(2,1)S(1)}, f32[768,128]{1,0:T(8,128)S(1)}, bf16[256,1152]{1,0:T(8,128)(2,1)}) custom-call(s32[289]{0:T(512)S(1)} %copy-done.9, s32[12,256]{1,0:T(8,128)S(1)} %add_select_fusion.target_of, bf16[32,192,1024]{2,1,0:T(8,128)(2,1)} %bitcast.22, ...), custom_call_target="tpu_custom_call" | custom-call | flops 6442450944 | bytes 8388608 | tf_op jit(solution)/shard_map/first_blocks/pallas_call | solution.py:347
  91.1 0.0 collective-permute-done.2.block
  91.1 0.0 copy-done.14
  91.1 10.5 %last_block.1 = (bf16[256,2048]{1,0:T(8,128)(2,1)S(1)}, bf16[1024,1024]{1,0:T(8,128)(2,1)S(1)}, bf16[1024,1024]{1,0:T(8,128)(2,1)S(1)}, f32[256,128]{1,0:T(8,128)S(1)}) custom-call(s32[1]{0:T(128)} %bitcast.8.core, bf16[2320,1024]{1,0:T(8,128)(2,1)S(1)} %get-tuple-element.53.passages, bf16[768,2048]{1,0:T(8,128)(2,1)S(1)} %get-tuple-element.64.before.refs_0_.refs_2_, ...), custom_call_target="tpu_custom_call" | custom-call | flops 6442450944 | bytes 8388608 | tf_op jit(solution)/shard_map/last_block/pallas_call | solution.py:452
  101.6 0.0 copy-start.5
  101.6 0.0 copy-start.7
  101.6 0.4 collective-permute-start.3
  102.0 3.0 %collective-permute-start.4 = (bf16[256,1152]{1,0:T(8,128)(2,1)}, bf16[256,1152]{1,0:T(8,128)(2,1)}, u32[]{:S(2)}, u32[]{:S(2)}) collective-permute-start(bf16[256,1152]{1,0:T(8,128)(2,1)} %get-tuple-element.66), channel_id=1, source_target_pairs={{0,96},{32,0},{64,32},{96,64},{1,97},{33,1},{65,33},{97,65},{2,98}... | collective-permute-start | bytes 1769480 | tf_op jit(solution)/shard_map/ppermute | solution.py:637
  105.0 2.3 %query_grads.2 = bf16[256,1152]{1,0:T(8,128)(2,1)} custom-call(bf16[2320,1024]{1,0:T(8,128)(2,1)S(1)} %get-tuple-element.53.passages, bf16[768,2048]{1,0:T(8,128)(2,1)S(1)} %get-tuple-element.64.before.refs_0_.refs_2_, f32[768,128]{1,0:T(8,128)S(1)} %get-tuple-element.58.refs_1_.refs_3_), custom_call_target="tpu_custom_call" | custom-call | flops 1073741824 | bytes 8388608 | tf_op jit(solution)/shard_map/query_grads/pallas_call | solution.py:491
  107.3 0.0 collective-permute-start.5
  107.3 0.0 collective-permute-done.3.other
  107.3 0.6 pair_sum.1
  107.9 1.4 copy-done.2
  109.3 6.6 %all-to-all-start = ((bf16[16,64,1024]{2,1,0:T(8,128)(2,1)}), bf16[16,64,1024]{2,1,0:T(8,128)(2,1)}, u32[]{:S(2)}, u32[]{:S(2)}) async-start(bf16[16,64,1024]{2,1,0:T(8,128)(2,1)} %bitcast.14), calls=%async_computation | async-start | bytes 4194304 | tf_op jit(solution)/shard_map/all_to_all | solution.py:663
  116.0 2.3 %copy-done.1 = bf16[2320,1024]{1,0:T(8,128)(2,1)S(1)} copy-done((bf16[2320,1024]{1,0:T(8,128)(2,1)S(1)}, bf16[2320,1024]{1,0:T(8,128)(2,1)}, u32[]{:S(2)}) %copy-start.1) | copy-done | bytes 4751384
  118.3 1.2 copy-done.6
  119.5 0.9 copy-done.8
  120.4 2.9 %query_grads.3 = (bf16[256,1152]{1,0:T(8,128)(2,1)S(1)}, bf16[256,1152]{1,0:T(8,128)(2,1)S(1)}) custom-call(bf16[2320,1024]{1,0:T(8,128)(2,1)S(1)} %copy-done.1, bf16[256,2048]{1,0:T(8,128)(2,1)S(1)} %copy-done.6, f32[256,128]{1,0:T(8,128)S(1)} %copy-done.8, bf16[768,2048]{1,0:T(8,128)(2,1)S(1)} %get-tuple-element.64.before.refs_0_.refs_2_, ...), custom_call_target="tpu_custom_call" | custom-call | flops 2147483648 | bytes 8388608 | tf_op jit(solution)/shard_map/query_grads/pallas_call | solution.py:491
  123.4 1.9 %collective-permute-start.6 = (bf16[256,1152]{1,0:T(8,128)(2,1)S(1)}, bf16[256,1152]{1,0:T(8,128)(2,1)S(1)}, u32[]{:S(2)}, u32[]{:S(2)}) collective-permute-start(bf16[256,1152]{1,0:T(8,128)(2,1)S(1)} %get-tuple-element.68), channel_id=1, source_target_pairs={{0,64},{32,96},{64,0},{96,32},{1,65},{33,97},{65,1},{97,33},{2,66}... | collective-permute-start | bytes 1769480 | tf_op jit(solution)/shard_map/ppermute | solution.py:637
  125.2 0.0 collective-permute-done.4.in1
  125.2 0.0 collective-permute-done.5.in3
  125.2 4.7 %restore_first.1.begun = bf16[1024,1152]{1,0:T(8,128)(2,1)S(1)} custom-call(s32[8,1024]{1,0:T(8,128)S(1)} %copy-done.17, bf16[256,1152]{1,0:T(8,128)(2,1)S(1)} %get-tuple-element.65.in0, bf16[256,1152]{1,0:T(8,128)(2,1)} %collective-permute-done.4.in1, bf16[256,1152]{1,0:T(8,128)(2,1)} %collective-permute-done.5.in3), custom_call_target="tpu_custom_call" | custom-call | flops 16106127360 | bytes 8388608 | tf_op jit(solution)/shard_map/restore_first/pallas_call | solution.py:579
  130.0 10.1 %collective-permute-done.6.in2 = bf16[256,1152]{1,0:T(8,128)(2,1)S(1)} collective-permute-done((bf16[256,1152]{1,0:T(8,128)(2,1)S(1)}, bf16[256,1152]{1,0:T(8,128)(2,1)S(1)}, u32[]{:S(2)}, u32[]{:S(2)}) %collective-permute-start.6) | collective-permute-done | bytes 589856 | tf_op jit(solution)/shard_map/ppermute | solution.py:637
  140.1 2.9 %restore_last.1 = (bf16[1024,1024]{1,0:T(8,128)(2,1)}, f32[1,1024]{1,0:T(1,128)}) custom-call(s32[8,1024]{1,0:T(8,128)S(1)} %copy-done.17, bf16[1024,1152]{1,0:T(8,128)(2,1)S(1)} %restore_first.1.begun, bf16[256,1152]{1,0:T(8,128)(2,1)S(1)} %collective-permute-done.6.in2), custom_call_target="tpu_custom_call" | custom-call | flops 1073741824 | bytes 8388608 | tf_op jit(solution)/shard_map/restore_last/pallas_call | solution.py:591
  143.0 4.2 %all-to-all-done.pieces = bf16[16,64,1024]{2,1,0:T(8,128)(2,1)} async-done(((bf16[16,64,1024]{2,1,0:T(8,128)(2,1)}), bf16[16,64,1024]{2,1,0:T(8,128)(2,1)}, u32[]{:S(2)}, u32[]{:S(2)}) %all-to-all-start) | async-done | bytes 2097184 | tf_op jit(solution)/shard_map/all_to_all | solution.py:663
  147.2 2.3 %sum_pieces.1 = bf16[64,1024]{1,0:T(8,128)(2,1)} custom-call(bf16[16,64,1024]{2,1,0:T(8,128)(2,1)} %all-to-all-done.pieces), custom_call_target="tpu_custom_call" | custom-call | flops 1048576 | bytes 8388608 | tf_op jit(solution)/shard_map/sum_pieces/pallas_call | solution.py:624
  (24 shorter events, 0.1 us)
Async XLA Ops:
  7.2 68.6 %all-gather.4.cloned.1.call-start = ((), (), s32[]{:S(2)}) async-start(), calls=%async_computation.1 | async-start | bytes 12976128 | tf_op jit(solution)/shard_map/all_gather | solution.py:644
  7.9 11.7 %copy-start.18 = (u32[128]{0:T(128)S(1)}, u32[128]{0:T(128)}, u32[]{:S(2)}) copy-start(u32[128]{0:T(128)} %constant.60) | copy-start | bytes 1540
  7.9 33.5 %copy-start.15 = (s32[1,1,1024]{2,1,0:T(1,128)S(1)}, s32[1,1,1024]{2,1,0:T(1,128)}, u32[]{:S(2)}) copy-start(s32[1,1,1024]{2,1,0:T(1,128)} %param.6) | copy-start | bytes 12292
  15.7 39.7 %collective-permute-start = (bf16[256,3072]{1,0:T(8,128)(2,1)}, bf16[256,3072]{1,0:T(8,128)(2,1)S(1)}, u32[]{:S(2)}, u32[]{:S(2)}) collective-permute-start(bf16[256,3072]{1,0:T(8,128)(2,1)} %get-tuple-element.41), channel_id=1, source_target_pairs={{0,32},{32,64},{64,96},{96,0},{1,33},{33,65},{65,97},{97,1},{2,34}... | collective-permute-start | bytes 4718600 | tf_op jit(solution)/shard_map/ppermute | solution.py:637
  17.3 38.0 %collective-permute-start.1 = (bf16[256,3072]{1,0:T(8,128)(2,1)}, bf16[256,3072]{1,0:T(8,128)(2,1)S(1)}, u32[]{:S(2)}, u32[]{:S(2)}) collective-permute-start(bf16[256,3072]{1,0:T(8,128)(2,1)} %get-tuple-element.42), channel_id=1, source_target_pairs={{0,96},{32,0},{64,32},{96,64},{1,97},{33,1},{65,33},{97,65},{2,98}... | collective-permute-start | bytes 4718600 | tf_op jit(solution)/shard_map/ppermute | solution.py:637
  41.5 2.2 %copy-start.10 = (bf16[1,1,1024,2048]{3,2,1,0:T(8,128)(2,1)S(1)}, bf16[1,1,1024,2048]{3,2,1,0:T(8,128)(2,1)}, u32[]{:S(2)}) copy-start(bf16[1,1,1024,2048]{3,2,1,0:T(8,128)(2,1)} %param.9) | copy-start | bytes 12582916
  43.6 1.6 %copy-start.11 = (bf16[1,1,1024,1024]{3,2,1,0:T(8,128)(2,1)S(1)}, bf16[1,1,1024,1024]{3,2,1,0:T(8,128)(2,1)}, u32[]{:S(2)}) copy-start(bf16[1,1,1024,1024]{3,2,1,0:T(8,128)(2,1)} %param.5) | copy-start | bytes 6291460
  45.2 0.8 copy-start.16
  52.4 1.1 copy-start.3
  53.5 1.1 copy-start.12
  55.4 35.7 %collective-permute-start.2 = (bf16[256,3072]{1,0:T(8,128)(2,1)}, bf16[256,3072]{1,0:T(8,128)(2,1)}, u32[]{:S(2)}, u32[]{:S(2)}) collective-permute-start(bf16[256,3072]{1,0:T(8,128)(2,1)} %copy-done.12), channel_id=1, source_target_pairs={{0,64},{32,96},{64,0},{96,32},{1,65},{33,97},{65,1},{97,33},{2,66}... | collective-permute-start | bytes 4718600 | tf_op jit(solution)/shard_map/ppermute | solution.py:637
  57.1 1.5 copy-start.4
  63.5 1.1 copy-start.13
  75.7 0.7 copy-start.9
  76.4 14.7 %copy-start.14 = (bf16[768,1024]{1,0:T(8,128)(2,1)S(1)}, bf16[768,1024]{1,0:T(8,128)(2,1)}, u32[]{:S(2)}) copy-start(bf16[768,1024]{1,0:T(8,128)(2,1)} %copy-done.13) | copy-start | bytes 4718596
  91.1 13.9 %copy-start = (bf16[2320,1024]{1,0:T(8,128)(2,1)}, bf16[2320,1024]{1,0:T(8,128)(2,1)S(1)}, u32[]{:S(2)}) copy-start(bf16[2320,1024]{1,0:T(8,128)(2,1)S(1)} %get-tuple-element.53.passages) | copy-start | bytes 14254084
  101.6 5.7 %copy-start.5 = (bf16[256,2048]{1,0:T(8,128)(2,1)}, bf16[256,2048]{1,0:T(8,128)(2,1)S(1)}, u32[]{:S(2)}) copy-start(bf16[256,2048]{1,0:T(8,128)(2,1)S(1)} %get-tuple-element.62.refs_0_) | copy-start | bytes 3145732
  101.6 5.7 %copy-start.7 = (f32[256,128]{1,0:T(8,128)}, f32[256,128]{1,0:T(8,128)S(1)}, u32[]{:S(2)}) copy-start(f32[256,128]{1,0:T(8,128)S(1)} %get-tuple-element.63.refs_1_) | copy-start | bytes 393220
  101.6 5.7 %collective-permute-start.3 = (bf16[1024,1024]{1,0:T(8,128)(2,1)S(1)}, bf16[1024,1024]{1,0:T(8,128)(2,1)S(1)}, u32[]{:S(2)}, u32[]{:S(2)}) collective-permute-start(bf16[1024,1024]{1,0:T(8,128)(2,1)S(1)} %get-tuple-element.60), channel_id=1, source_target_pairs={{0,1},{1,0},{2,3},{3,2},{4,5},{5,4},{6,7},{7,6},{8,9},{9,8},{10,11... | collective-permute-start | bytes 6291464 | tf_op jit(solution)/shard_map/ppermute | solution.py:658
  102.0 23.2 %collective-permute-start.4 = (bf16[256,1152]{1,0:T(8,128)(2,1)}, bf16[256,1152]{1,0:T(8,128)(2,1)}, u32[]{:S(2)}, u32[]{:S(2)}) collective-permute-start(bf16[256,1152]{1,0:T(8,128)(2,1)} %get-tuple-element.66), channel_id=1, source_target_pairs={{0,96},{32,0},{64,32},{96,64},{1,97},{33,1},{65,33},{97,65},{2,98}... | collective-permute-start | bytes 1769480 | tf_op jit(solution)/shard_map/ppermute | solution.py:637
  107.3 17.9 %collective-permute-start.5 = (bf16[256,1152]{1,0:T(8,128)(2,1)}, bf16[256,1152]{1,0:T(8,128)(2,1)}, u32[]{:S(2)}, u32[]{:S(2)}) collective-permute-start(bf16[256,1152]{1,0:T(8,128)(2,1)} %query_grads.2), channel_id=1, source_target_pairs={{0,32},{32,64},{64,96},{96,0},{1,33},{33,65},{65,97},{97,1},{2,34}... | collective-permute-start | bytes 1769480 | tf_op jit(solution)/shard_map/ppermute | solution.py:637
  107.9 1.4 copy-start.2
  109.3 37.9 %all-to-all-start = ((bf16[16,64,1024]{2,1,0:T(8,128)(2,1)}), bf16[16,64,1024]{2,1,0:T(8,128)(2,1)}, u32[]{:S(2)}, u32[]{:S(2)}) async-start(bf16[16,64,1024]{2,1,0:T(8,128)(2,1)} %bitcast.14), calls=%async_computation | async-start | bytes 4194304 | tf_op jit(solution)/shard_map/all_to_all | solution.py:663
  116.0 2.3 %copy-start.1 = (bf16[2320,1024]{1,0:T(8,128)(2,1)S(1)}, bf16[2320,1024]{1,0:T(8,128)(2,1)}, u32[]{:S(2)}) copy-start(bf16[2320,1024]{1,0:T(8,128)(2,1)} %copy-done) | copy-start | bytes 14254084
  118.3 1.2 copy-start.6
  119.5 0.9 copy-start.8
  120.4 4.8 %copy-start.17 = (s32[8,1024]{1,0:T(8,128)S(1)}, s32[8,1024]{1,0:T(8,128)}, u32[]{:S(2)}) copy-start(s32[8,1024]{1,0:T(8,128)} %get-tuple-element.37.slot_in.slot) | copy-start | bytes 98308
  123.4 16.7 %collective-permute-start.6 = (bf16[256,1152]{1,0:T(8,128)(2,1)S(1)}, bf16[256,1152]{1,0:T(8,128)(2,1)S(1)}, u32[]{:S(2)}, u32[]{:S(2)}) collective-permute-start(bf16[256,1152]{1,0:T(8,128)(2,1)S(1)} %get-tuple-element.68), channel_id=1, source_target_pairs={{0,64},{32,96},{64,0},{96,32},{1,65},{33,97},{65,1},{97,33},{2,66}... | collective-permute-start | bytes 1769480 | tf_op jit(solution)/shard_map/ppermute | solution.py:637
Sparse Core Ops, SparseCore 0:
  10.3 65.4 all-gather.3
where the time goes:
time: 157 us; the launch traced here: 156 us
  Pallas kernels  59.9 us (38%)
  waiting for transfers between devices  26 us (17%)
  blocking collectives  18.4 us (12%)
  local copies, waits for them, and re-layouts  17.9 us (11%)
  starting transfers between devices  17 us (11%)
  between operations  15.6 us (10%)
    all_gather x1, blocking collectives, on_device(): holder_counts = lax.all_gather(held_counts[0], group, axis=0, tiled=True)  18.4 us
    unnamed x41, local copies, waits for them, and re-layouts  17.3 us
    pallas_call x1, Pallas kernels, first_blocks(): call(first_kernel, 'first_blocks', [smem, vmem, hbm, hbm], [(vmem, (rows,...  14.6 us
    pallas_call x2, Pallas kernels, sort_rows(): call(functools.partial(sort_kernel, first), 'sort_first' if first else 's...  14.1 us
    all_gather x1, waiting for transfers between devices, on_device(): all_raw = lax.all_gather(raw_passages[0], group, axis=0, tiled=True)  11.1 us
    pallas_call x1, Pallas kernels, last_block(): call(last_kernel, 'last_block', [smem] + [vmem] * 3 + [hbm], [(vmem, (per...  10.5 us
    ppermute x6, waiting for transfers between devices, shift(): return lax.ppermute(array, 'x', pairs)  10.1 us
    ppermute x6, starting transfers between devices, shift(): return lax.ppermute(array, 'x', pairs)  9.93 us
  transfers between devices with their start and end apart: 9, of which 3 were waited for; matrix products, arithmetic and copies ran while one was open for 2% of the time, Pallas kernels for 30%

commit v1 on v0

--- a/solution.py
+++ b/solution.py
@@ -282,8 +282,8 @@
     groups = chunk_list[3 * chunk_count]
 
     def start_group(g, carry):
-        for c in range(group_chunks):
-            raw_copy(g * group_chunks + c).start()
+        for c in range(2 * group_chunks):
+            raw_copy(2 * g * group_chunks + c).start()
         return carry
 
     lax.fori_loop(0, groups, start_group, 0)
@@ -299,18 +299,24 @@
         copy.start()
     passages[pl.ds(0, 16), :] = jnp.zeros((16, width), jnp.bfloat16)
 
-    def place(g, carry):
-        for c in range(group_chunks):
-            raw_copy(g * group_chunks + c).wait()
-        start = pl.multiple_of((chunk_list[2 * chunk_count + g * group_chunks] // 16) * 16, 16)
-        target = lax.broadcasted_iota(jnp.int32, (window, group_rows), 0)
-        hit = target == target_of[pl.ds(g, 1), :] - start
-        chosen = hit.astype(jnp.float32).astype(jnp.bfloat16)
-        chunks = raw_v[pl.ds(g * group_chunks, group_chunks)].reshape(group_rows, width)
-        moved = jnp.dot(chosen, chunks, preferred_element_type=jnp.float32).astype(jnp.bfloat16)
-        head = passages[pl.ds(start, 16), :]
-        passages[pl.ds(start, 16), :] = head + moved[:16]
-        passages[pl.ds(start + 16, window - 16), :] = moved[16:]
+    def place(pair, carry):
+        ready = []
+        for g in (2 * pair, 2 * pair + 1):
+            for c in range(group_chunks):
+                raw_copy(g * group_chunks + c).wait()
+        for g in (2 * pair, 2 * pair + 1):
+            first = chunk_list[2 * chunk_count + g * group_chunks]
+            start = pl.multiple_of((first // 16) * 16, 16)
+            target = lax.broadcasted_iota(jnp.int32, (window, group_rows), 0)
+            hit = target == target_of[pl.ds(g, 1), :] - start
+            chosen = hit.astype(jnp.float32).astype(jnp.bfloat16)
+            chunks = raw_v[pl.ds(g * group_chunks, group_chunks)].reshape(group_rows, width)
+            moved = jnp.dot(chosen, chunks, preferred_element_type=jnp.float32)
+            ready.append((start, moved.astype(jnp.bfloat16)))
+        for start, moved in ready:
+            head = passages[pl.ds(start, 16), :]
+            passages[pl.ds(start, 16), :] = head + moved[:16]
+            passages[pl.ds(start + 16, window - 16), :] = moved[16:]
         return carry
 
     lax.fori_loop(0, groups, place, 0)
@@ -385,7 +391,7 @@
     used = pick(jnp.minimum(counts[None, :] - row, chunk_rows))
     place = jnp.where(used > 0, pick(offsets[None, :] + row), passages_all)
     slots = jnp.arange(chunk_rows)[None, :]
-    groups = (jnp.sum(number) + group_chunks - 1) // group_chunks
+    groups = (jnp.sum(number) + 2 * group_chunks - 1) // (2 * group_chunks)
     targets = jnp.where(slots < used[:, None], place[:, None] + slots, -1)
     return (
         jnp.concatenate([holder, pick(row), place, groups[None]]).astype(jnp.int32),
@@ -607,13 +613,18 @@
 
 
 def sum_kernel(pieces, out, held, sems):
-    copies = []
+    def read(i, j):
+        rows, some = pl.ds(16 * i, 16), pl.ds(4 * j, 4)
+        return pltpu.make_async_copy(
+            pieces.at[some, rows], held.at[some, rows], sems.at[4 * i + j]
+        )
+
     for i in range(4):
-        rows = pl.ds(16 * i, 16)
-        copies.append(pltpu.make_async_copy(pieces.at[:, rows], held.at[:, rows], sems.at[i]))
-        copies[-1].start()
-    for i, copy in enumerate(copies):
-        copy.wait()
+        for j in range(4):
+            read(i, j).start()
+    for i in range(4):
+        for j in range(4):
+            read(i, j).wait()
         total = held[0, 16 * i : 16 * (i + 1), :].astype(jnp.float32)
         for j in range(1, pieces.shape[0]):
             total = total + held[j, 16 * i : 16 * (i + 1), :].astype(jnp.float32)
@@ -626,7 +637,7 @@
         "sum_pieces",
         [hbm],
         [(vmem, (64, width), jnp.bfloat16)],
-        [pltpu.VMEM(pieces.shape, jnp.bfloat16), pltpu.SemaphoreType.DMA((4,))],
+        [pltpu.VMEM(pieces.shape, jnp.bfloat16), pltpu.SemaphoreType.DMA((16,))],
         8,
         mib,
     )(pieces)[0]

time: 157 us -> 157 us (level)
  transfers between devices with their start and end apart: 9 -> 9, of which waited for: 3 -> 4; matrix products, arithmetic and copies ran while one was open for 2% -> 2% of each run, Pallas kernels for 30% -> 30%
where the time goes in v1:
time: 157 us
  Pallas kernels  59.8 us (38%)
  waiting for transfers between devices  26.2 us (17%)
  blocking collectives  18.4 us (12%)
  local copies, waits for them, and re-layouts  17.9 us (11%)
  starting transfers between devices  17.1 us (11%)
  between operations  15.6 us (10%)
    all_gather x1, blocking collectives, on_device(): holder_counts = lax.all_gather(held_counts[0], group, axis=0, tiled=True)  18.4 us
    unnamed x41, local copies, waits for them, and re-layouts  17.3 us
    pallas_call x1, Pallas kernels, first_blocks(): call(first_kernel, 'first_blocks', [smem, vmem, hbm, hbm], [(vmem, (rows,...  14.3 us
    pallas_call x2, Pallas kernels, sort_rows(): call(functools.partial(sort_kernel, first), 'sort_first' if first else 's...  14.1 us
    all_gather x1, waiting for transfers between devices, on_device(): all_raw = lax.all_gather(raw_passages[0], group, axis=0, tiled=True)  11.1 us
    pallas_call x1, Pallas kernels, last_block(): call(last_kernel, 'last_block', [smem] + [vmem] * 3 + [hbm], [(vmem, (per...  10.5 us
    ppermute x6, waiting for transfers between devices, shift(): return lax.ppermute(array, 'x', pairs)  10.3 us
    ppermute x6, starting transfers between devices, shift(): return lax.ppermute(array, 'x', pairs)  9.63 us
  transfers between devices with their start and end apart: 9, of which 4 were waited for; matrix products, arithmetic and copies ran while one was open for 2% of the time, Pallas kernels for 30%

profile of v1, /device:TPU:0, one launch (start us, length us, event | category | flops | bytes accessed | tf_op | source)
XLA Modules:
  0.0 156.5 jit_solution(4319869357300853339)
XLA Ops:
  7.2 0.0 all-gather.4.cloned.1.call-start
  7.2 0.7 all-gather.4.cloned.1.call-update
  7.9 0.0 copy-start.18
  7.9 7.8 %sort_first.1 = (bf16[256,3072]{1,0:T(8,128)(2,1)}, bf16[256,3072]{1,0:T(8,128)(2,1)}, s32[8,1024]{1,0:T(8,128)}) custom-call(s32[1]{0:T(128)} %bitcast.here, s32[1,1024]{1,0:T(1,128)} %bitcast.19, s32[1,1024]{1,0:T(1,128)} %bitcast.20, bf16[1024,1024]{1,0:T(8,128)(2,1)} %bitcast.17, bf16[1024,2048]{1,0:T(8,128)(2,1)} %bitcast.15), custom_call_target="tpu_custom_call" | custom-call | flops 3221225472 | bytes 8388608 | tf_op jit(solution)/shard_map/sort_first/pallas_call | solution.py:122
  15.7 1.6 %collective-permute-start = (bf16[256,3072]{1,0:T(8,128)(2,1)}, bf16[256,3072]{1,0:T(8,128)(2,1)S(1)}, u32[]{:S(2)}, u32[]{:S(2)}) collective-permute-start(bf16[256,3072]{1,0:T(8,128)(2,1)} %get-tuple-element.41), channel_id=1, source_target_pairs={{0,32},{32,64},{64,96},{96,0},{1,33},{33,65},{65,97},{97,1},{2,34}... | collective-permute-start | bytes 4718600 | tf_op jit(solution)/shard_map/ppermute | solution.py:648
  17.3 1.7 %collective-permute-start.1 = (bf16[256,3072]{1,0:T(8,128)(2,1)}, bf16[256,3072]{1,0:T(8,128)(2,1)S(1)}, u32[]{:S(2)}, u32[]{:S(2)}) collective-permute-start(bf16[256,3072]{1,0:T(8,128)(2,1)} %get-tuple-element.42), channel_id=1, source_target_pairs={{0,96},{32,0},{64,32},{96,64},{1,97},{33,1},{65,33},{97,65},{2,98}... | collective-permute-start | bytes 4718600 | tf_op jit(solution)/shard_map/ppermute | solution.py:648
  19.6 0.0 copy-done.18
  19.7 0.6 dynamic-slice
  20.2 0.7 bitcast_dynamic-update-slice_fusion
  20.9 18.4 %all-reduce = s32[32]{0:T(128)S(1)} all-reduce(s32[32]{0:T(128)S(1)} %bitcast_dynamic-update-slice_fusion), channel_id=2, replica_groups=mesh['x'=4,'y'=4,'z'=4,'c'=2] {'y','z','c'}, use_global_device_ids=true, to_apply=%add | all-reduce | flops 32 | bytes 256 | tf_op jit(solution)/shard_map/all_gather | solution.py:661
  39.3 0.6 fusion.1
  40.6 0.1 select_reduce_fusion.1
  40.8 0.1 add.58
  40.8 0.1 select_reduce_fusion.4
  40.9 0.1 lt.51
  41.0 0.1 reduce_sum.72
  41.1 0.1 lt.52
  41.2 0.1 lt.53
  41.3 0.1 add.60
  41.4 0.1 add.61
  41.5 0.0 copy-start.10
  41.5 2.2 %copy-done.10 = bf16[1,1,1024,2048]{3,2,1,0:T(8,128)(2,1)S(1)} copy-done((bf16[1,1,1024,2048]{3,2,1,0:T(8,128)(2,1)S(1)}, bf16[1,1,1024,2048]{3,2,1,0:T(8,128)(2,1)}, u32[]{:S(2)}) %copy-start.10) | copy-done | bytes 4194328
  43.6 1.6 %copy-done.11 = bf16[1,1,1024,1024]{3,2,1,0:T(8,128)(2,1)S(1)} copy-done((bf16[1,1,1024,1024]{3,2,1,0:T(8,128)(2,1)S(1)}, bf16[1,1,1024,1024]{3,2,1,0:T(8,128)(2,1)}, u32[]{:S(2)}) %copy-start.11) | copy-done | bytes 2097176
  45.2 0.8 copy-done.16
  46.0 6.4 %sort_rest.1 = (bf16[256,3072]{1,0:T(8,128)(2,1)S(1)}, bf16[256,3072]{1,0:T(8,128)(2,1)S(1)}, s32[8,128]{1,0:T(8,128)}) custom-call(s32[1]{0:T(128)} %bitcast.here, s32[1,1024]{1,0:T(1,128)S(1)} %bitcast.21, s32[8,1024]{1,0:T(8,128)S(1)} %copy-done.16, bf16[1024,1024]{1,0:T(8,128)(2,1)S(1)} %bitcast.18, bf16[1024,2048]{1,0:T(8,128)(2,1)S(1)} %bitcast.16), custom_call_target="tpu_custom_call" | custom-call | flops 3221225472 | bytes 8388608 | tf_op jit(solution)/shard_map/sort_rest/pallas_call | solution.py:122
  52.4 0.0 copy-start.3
  52.4 1.1 copy-done.3
  53.6 1.1 copy-done.12
  54.7 0.7 pad_add_fusion.chunk_list
  55.3 0.0 collective-permute-done.in1
  55.3 0.0 collective-permute-done.1.in2
  55.4 1.8 %collective-permute-start.2 = (bf16[256,3072]{1,0:T(8,128)(2,1)}, bf16[256,3072]{1,0:T(8,128)(2,1)}, u32[]{:S(2)}, u32[]{:S(2)}) collective-permute-start(bf16[256,3072]{1,0:T(8,128)(2,1)} %copy-done.12), channel_id=1, source_target_pairs={{0,64},{32,96},{64,0},{96,32},{1,65},{33,97},{65,1},{97,33},{2,66}... | collective-permute-start | bytes 4718600 | tf_op jit(solution)/shard_map/ppermute | solution.py:648
  57.1 1.5 copy-done.4
  58.7 4.8 %teacher_rows.1 = (bf16[6144,2048]{1,0:T(8,128)(2,1)}, bf16[768,1024]{1,0:T(8,128)(2,1)S(1)}) custom-call(bf16[256,3072]{1,0:T(8,128)(2,1)S(1)} %copy-done.4, bf16[256,3072]{1,0:T(8,128)(2,1)S(1)} %collective-permute-done.in1, bf16[256,3072]{1,0:T(8,128)(2,1)S(1)} %collective-permute-done.1.in2), custom_call_target="tpu_custom_call" | custom-call | flops 1048576 | bytes 8388608 | tf_op jit(solution)/shard_map/teacher_rows/pallas_call | solution.py:229
  63.5 0.0 copy-start.13
  63.5 1.1 copy-done.13
  64.7 11.1 %all-gather.4.cloned.1.call-done = bf16[32,1,192,1024]{3,2,1,0:T(8,128)(2,1)} async-done(((bf16[1,1,192,1024]{3,2,1,0:T(8,128)(2,1)}), bf16[32,1,192,1024]{3,2,1,0:T(8,128)(2,1)}) %all-gather.4.cloned.1.call-update) | async-done | bytes 12582928 | tf_op jit(solution)/shard_map/all_gather | solution.py:655
  75.7 0.7 copy-done.9
  76.4 14.3 %first_blocks.1 = (bf16[768,2048]{1,0:T(8,128)(2,1)S(1)}, bf16[2320,1024]{1,0:T(8,128)(2,1)S(1)}, f32[768,128]{1,0:T(8,128)S(1)}, bf16[256,1152]{1,0:T(8,128)(2,1)}) custom-call(s32[289]{0:T(512)S(1)} %copy-done.9, s32[12,256]{1,0:T(8,128)S(1)} %add_select_fusion.target_of, bf16[32,192,1024]{2,1,0:T(8,128)(2,1)} %bitcast.22, ...), custom_call_target="tpu_custom_call" | custom-call | flops 6442450944 | bytes 8388608 | tf_op jit(solution)/shard_map/first_blocks/pallas_call | solution.py:353
  90.8 0.2 collective-permute-done.2.block
  90.9 0.0 copy-done.14
  90.9 10.5 %last_block.1 = (bf16[256,2048]{1,0:T(8,128)(2,1)S(1)}, bf16[1024,1024]{1,0:T(8,128)(2,1)S(1)}, bf16[1024,1024]{1,0:T(8,128)(2,1)S(1)}, f32[256,128]{1,0:T(8,128)S(1)}) custom-call(s32[1]{0:T(128)} %bitcast.8.core, bf16[2320,1024]{1,0:T(8,128)(2,1)S(1)} %get-tuple-element.53.passages, bf16[768,2048]{1,0:T(8,128)(2,1)S(1)} %get-tuple-element.64.before.refs_0_.refs_2_, ...), custom_call_target="tpu_custom_call" | custom-call | flops 6442450944 | bytes 8388608 | tf_op jit(solution)/shard_map/last_block/pallas_call | solution.py:458
  101.5 0.0 copy-start.5
  101.5 0.0 copy-start.7
  101.5 0.2 collective-permute-start.3
  101.7 2.7 %collective-permute-start.4 = (bf16[256,1152]{1,0:T(8,128)(2,1)}, bf16[256,1152]{1,0:T(8,128)(2,1)}, u32[]{:S(2)}, u32[]{:S(2)}) collective-permute-start(bf16[256,1152]{1,0:T(8,128)(2,1)} %get-tuple-element.66), channel_id=1, source_target_pairs={{0,96},{32,0},{64,32},{96,64},{1,97},{33,1},{65,33},{97,65},{2,98}... | collective-permute-start | bytes 1769480 | tf_op jit(solution)/shard_map/ppermute | solution.py:648
  104.4 2.3 %query_grads.2 = bf16[256,1152]{1,0:T(8,128)(2,1)} custom-call(bf16[2320,1024]{1,0:T(8,128)(2,1)S(1)} %get-tuple-element.53.passages, bf16[768,2048]{1,0:T(8,128)(2,1)S(1)} %get-tuple-element.64.before.refs_0_.refs_2_, f32[768,128]{1,0:T(8,128)S(1)} %get-tuple-element.58.refs_1_.refs_3_), custom_call_target="tpu_custom_call" | custom-call | flops 1073741824 | bytes 8388608 | tf_op jit(solution)/shard_map/query_grads/pallas_call | solution.py:497
  106.7 0.0 collective-permute-start.5
  106.7 0.0 collective-permute-done.3.other
  106.7 0.6 pair_sum.1
  107.3 1.4 copy-done.2
  108.7 7.3 %all-to-all-start = ((bf16[16,64,1024]{2,1,0:T(8,128)(2,1)}), bf16[16,64,1024]{2,1,0:T(8,128)(2,1)}, u32[]{:S(2)}, u32[]{:S(2)}) async-start(bf16[16,64,1024]{2,1,0:T(8,128)(2,1)} %bitcast.14), calls=%async_computation | async-start | bytes 4194304 | tf_op jit(solution)/shard_map/all_to_all | solution.py:674
  116.0 2.3 %copy-done.1 = bf16[2320,1024]{1,0:T(8,128)(2,1)S(1)} copy-done((bf16[2320,1024]{1,0:T(8,128)(2,1)S(1)}, bf16[2320,1024]{1,0:T(8,128)(2,1)}, u32[]{:S(2)}) %copy-start.1) | copy-done | bytes 4751384
  118.3 1.2 copy-done.6
  119.5 0.9 copy-done.8
  120.4 2.9 %query_grads.3 = (bf16[256,1152]{1,0:T(8,128)(2,1)S(1)}, bf16[256,1152]{1,0:T(8,128)(2,1)S(1)}) custom-call(bf16[2320,1024]{1,0:T(8,128)(2,1)S(1)} %copy-done.1, bf16[256,2048]{1,0:T(8,128)(2,1)S(1)} %copy-done.6, f32[256,128]{1,0:T(8,128)S(1)} %copy-done.8, bf16[768,2048]{1,0:T(8,128)(2,1)S(1)} %get-tuple-element.64.before.refs_0_.refs_2_, ...), custom_call_target="tpu_custom_call" | custom-call | flops 2147483648 | bytes 8388608 | tf_op jit(solution)/shard_map/query_grads/pallas_call | solution.py:497
  123.4 1.9 %collective-permute-start.6 = (bf16[256,1152]{1,0:T(8,128)(2,1)S(1)}, bf16[256,1152]{1,0:T(8,128)(2,1)S(1)}, u32[]{:S(2)}, u32[]{:S(2)}) collective-permute-start(bf16[256,1152]{1,0:T(8,128)(2,1)S(1)} %get-tuple-element.68), channel_id=1, source_target_pairs={{0,64},{32,96},{64,0},{96,32},{1,65},{33,97},{65,1},{97,33},{2,66}... | collective-permute-start | bytes 1769480 | tf_op jit(solution)/shard_map/ppermute | solution.py:648
  125.2 0.0 collective-permute-done.4.in1
  125.2 0.0 collective-permute-done.5.in3
  125.2 4.7 %restore_first.1.begun = bf16[1024,1152]{1,0:T(8,128)(2,1)S(1)} custom-call(s32[8,1024]{1,0:T(8,128)S(1)} %copy-done.17, bf16[256,1152]{1,0:T(8,128)(2,1)S(1)} %get-tuple-element.65.in0, bf16[256,1152]{1,0:T(8,128)(2,1)} %collective-permute-done.4.in1, bf16[256,1152]{1,0:T(8,128)(2,1)} %collective-permute-done.5.in3), custom_call_target="tpu_custom_call" | custom-call | flops 16106127360 | bytes 8388608 | tf_op jit(solution)/shard_map/restore_first/pallas_call | solution.py:585
  130.0 10.1 %collective-permute-done.6.in2 = bf16[256,1152]{1,0:T(8,128)(2,1)S(1)} collective-permute-done((bf16[256,1152]{1,0:T(8,128)(2,1)S(1)}, bf16[256,1152]{1,0:T(8,128)(2,1)S(1)}, u32[]{:S(2)}, u32[]{:S(2)}) %collective-permute-start.6) | collective-permute-done | bytes 589856 | tf_op jit(solution)/shard_map/ppermute | solution.py:648
  140.1 2.9 %restore_last.1 = (bf16[1024,1024]{1,0:T(8,128)(2,1)}, f32[1,1024]{1,0:T(1,128)}) custom-call(s32[8,1024]{1,0:T(8,128)S(1)} %copy-done.17, bf16[1024,1152]{1,0:T(8,128)(2,1)S(1)} %restore_first.1.begun, bf16[256,1152]{1,0:T(8,128)(2,1)S(1)} %collective-permute-done.6.in2), custom_call_target="tpu_custom_call" | custom-call | flops 1073741824 | bytes 8388608 | tf_op jit(solution)/shard_map/restore_last/pallas_call | solution.py:597
  143.0 4.2 %all-to-all-done.pieces = bf16[16,64,1024]{2,1,0:T(8,128)(2,1)} async-done(((bf16[16,64,1024]{2,1,0:T(8,128)(2,1)}), bf16[16,64,1024]{2,1,0:T(8,128)(2,1)}, u32[]{:S(2)}, u32[]{:S(2)}) %all-to-all-start) | async-done | bytes 2097184 | tf_op jit(solution)/shard_map/all_to_all | solution.py:674
  147.2 2.5 %sum_pieces.1 = bf16[64,1024]{1,0:T(8,128)(2,1)} custom-call(bf16[16,64,1024]{2,1,0:T(8,128)(2,1)} %all-to-all-done.pieces), custom_call_target="tpu_custom_call" | custom-call | flops 1048576 | bytes 8388608 | tf_op jit(solution)/shard_map/sum_pieces/pallas_call | solution.py:635
  (24 shorter events, 0.1 us)
Async XLA Ops:
  7.2 68.6 %all-gather.4.cloned.1.call-start = ((), (), s32[]{:S(2)}) async-start(), calls=%async_computation.1 | async-start | bytes 12976128 | tf_op jit(solution)/shard_map/all_gather | solution.py:655
  7.9 11.7 %copy-start.18 = (u32[128]{0:T(128)S(1)}, u32[128]{0:T(128)}, u32[]{:S(2)}) copy-start(u32[128]{0:T(128)} %constant.60) | copy-start | bytes 1540
  7.9 33.5 %copy-start.15 = (s32[1,1,1024]{2,1,0:T(1,128)S(1)}, s32[1,1,1024]{2,1,0:T(1,128)}, u32[]{:S(2)}) copy-start(s32[1,1,1024]{2,1,0:T(1,128)} %param.6) | copy-start | bytes 12292
  15.7 39.7 %collective-permute-start = (bf16[256,3072]{1,0:T(8,128)(2,1)}, bf16[256,3072]{1,0:T(8,128)(2,1)S(1)}, u32[]{:S(2)}, u32[]{:S(2)}) collective-permute-start(bf16[256,3072]{1,0:T(8,128)(2,1)} %get-tuple-element.41), channel_id=1, source_target_pairs={{0,32},{32,64},{64,96},{96,0},{1,33},{33,65},{65,97},{97,1},{2,34}... | collective-permute-start | bytes 4718600 | tf_op jit(solution)/shard_map/ppermute | solution.py:648
  17.3 38.0 %collective-permute-start.1 = (bf16[256,3072]{1,0:T(8,128)(2,1)}, bf16[256,3072]{1,0:T(8,128)(2,1)S(1)}, u32[]{:S(2)}, u32[]{:S(2)}) collective-permute-start(bf16[256,3072]{1,0:T(8,128)(2,1)} %get-tuple-element.42), channel_id=1, source_target_pairs={{0,96},{32,0},{64,32},{96,64},{1,97},{33,1},{65,33},{97,65},{2,98}... | collective-permute-start | bytes 4718600 | tf_op jit(solution)/shard_map/ppermute | solution.py:648
  41.5 2.2 %copy-start.10 = (bf16[1,1,1024,2048]{3,2,1,0:T(8,128)(2,1)S(1)}, bf16[1,1,1024,2048]{3,2,1,0:T(8,128)(2,1)}, u32[]{:S(2)}) copy-start(bf16[1,1,1024,2048]{3,2,1,0:T(8,128)(2,1)} %param.9) | copy-start | bytes 12582916
  43.6 1.6 %copy-start.11 = (bf16[1,1,1024,1024]{3,2,1,0:T(8,128)(2,1)S(1)}, bf16[1,1,1024,1024]{3,2,1,0:T(8,128)(2,1)}, u32[]{:S(2)}) copy-start(bf16[1,1,1024,1024]{3,2,1,0:T(8,128)(2,1)} %param.5) | copy-start | bytes 6291460
  45.2 0.8 copy-start.16
  52.4 1.1 copy-start.3
  53.5 1.1 copy-start.12
  55.4 35.6 %collective-permute-start.2 = (bf16[256,3072]{1,0:T(8,128)(2,1)}, bf16[256,3072]{1,0:T(8,128)(2,1)}, u32[]{:S(2)}, u32[]{:S(2)}) collective-permute-start(bf16[256,3072]{1,0:T(8,128)(2,1)} %copy-done.12), channel_id=1, source_target_pairs={{0,64},{32,96},{64,0},{96,32},{1,65},{33,97},{65,1},{97,33},{2,66}... | collective-permute-start | bytes 4718600 | tf_op jit(solution)/shard_map/ppermute | solution.py:648
  57.1 1.5 copy-start.4
  63.5 1.1 copy-start.13
  75.7 0.7 copy-start.9
  76.4 14.5 %copy-start.14 = (bf16[768,1024]{1,0:T(8,128)(2,1)S(1)}, bf16[768,1024]{1,0:T(8,128)(2,1)}, u32[]{:S(2)}) copy-start(bf16[768,1024]{1,0:T(8,128)(2,1)} %copy-done.13) | copy-start | bytes 4718596
  90.8 13.6 %copy-start = (bf16[2320,1024]{1,0:T(8,128)(2,1)}, bf16[2320,1024]{1,0:T(8,128)(2,1)S(1)}, u32[]{:S(2)}) copy-start(bf16[2320,1024]{1,0:T(8,128)(2,1)S(1)} %get-tuple-element.53.passages) | copy-start | bytes 14254084
  101.5 5.2 %copy-start.5 = (bf16[256,2048]{1,0:T(8,128)(2,1)}, bf16[256,2048]{1,0:T(8,128)(2,1)S(1)}, u32[]{:S(2)}) copy-start(bf16[256,2048]{1,0:T(8,128)(2,1)S(1)} %get-tuple-element.62.refs_0_) | copy-start | bytes 3145732
  101.5 5.2 %copy-start.7 = (f32[256,128]{1,0:T(8,128)}, f32[256,128]{1,0:T(8,128)S(1)}, u32[]{:S(2)}) copy-start(f32[256,128]{1,0:T(8,128)S(1)} %get-tuple-element.63.refs_1_) | copy-start | bytes 393220
  101.5 5.2 %collective-permute-start.3 = (bf16[1024,1024]{1,0:T(8,128)(2,1)S(1)}, bf16[1024,1024]{1,0:T(8,128)(2,1)S(1)}, u32[]{:S(2)}, u32[]{:S(2)}) collective-permute-start(bf16[1024,1024]{1,0:T(8,128)(2,1)S(1)} %get-tuple-element.60), channel_id=1, source_target_pairs={{0,1},{1,0},{2,3},{3,2},{4,5},{5,4},{6,7},{7,6},{8,9},{9,8},{10,11... | collective-permute-start | bytes 6291464 | tf_op jit(solution)/shard_map/ppermute | solution.py:669
  101.7 23.5 %collective-permute-start.4 = (bf16[256,1152]{1,0:T(8,128)(2,1)}, bf16[256,1152]{1,0:T(8,128)(2,1)}, u32[]{:S(2)}, u32[]{:S(2)}) collective-permute-start(bf16[256,1152]{1,0:T(8,128)(2,1)} %get-tuple-element.66), channel_id=1, source_target_pairs={{0,96},{32,0},{64,32},{96,64},{1,97},{33,1},{65,33},{97,65},{2,98}... | collective-permute-start | bytes 1769480 | tf_op jit(solution)/shard_map/ppermute | solution.py:648
  106.7 18.5 %collective-permute-start.5 = (bf16[256,1152]{1,0:T(8,128)(2,1)}, bf16[256,1152]{1,0:T(8,128)(2,1)}, u32[]{:S(2)}, u32[]{:S(2)}) collective-permute-start(bf16[256,1152]{1,0:T(8,128)(2,1)} %query_grads.2), channel_id=1, source_target_pairs={{0,32},{32,64},{64,96},{96,0},{1,33},{33,65},{65,97},{97,1},{2,34}... | collective-permute-start | bytes 1769480 | tf_op jit(solution)/shard_map/ppermute | solution.py:648
  107.3 1.4 copy-start.2
  108.7 38.5 %all-to-all-start = ((bf16[16,64,1024]{2,1,0:T(8,128)(2,1)}), bf16[16,64,1024]{2,1,0:T(8,128)(2,1)}, u32[]{:S(2)}, u32[]{:S(2)}) async-start(bf16[16,64,1024]{2,1,0:T(8,128)(2,1)} %bitcast.14), calls=%async_computation | async-start | bytes 4194304 | tf_op jit(solution)/shard_map/all_to_all | solution.py:674
  116.0 2.3 %copy-start.1 = (bf16[2320,1024]{1,0:T(8,128)(2,1)S(1)}, bf16[2320,1024]{1,0:T(8,128)(2,1)}, u32[]{:S(2)}) copy-start(bf16[2320,1024]{1,0:T(8,128)(2,1)} %copy-done) | copy-start | bytes 14254084
  118.3 1.2 copy-start.6
  119.5 0.9 copy-start.8
  120.4 4.8 %copy-start.17 = (s32[8,1024]{1,0:T(8,128)S(1)}, s32[8,1024]{1,0:T(8,128)}, u32[]{:S(2)}) copy-start(s32[8,1024]{1,0:T(8,128)} %get-tuple-element.37.slot_in.slot) | copy-start | bytes 98308
  123.4 16.7 %collective-permute-start.6 = (bf16[256,1152]{1,0:T(8,128)(2,1)S(1)}, bf16[256,1152]{1,0:T(8,128)(2,1)S(1)}, u32[]{:S(2)}, u32[]{:S(2)}) collective-permute-start(bf16[256,1152]{1,0:T(8,128)(2,1)S(1)} %get-tuple-element.68), channel_id=1, source_target_pairs={{0,64},{32,96},{64,0},{96,32},{1,65},{33,97},{65,1},{97,33},{2,66}... | collective-permute-start | bytes 1769480 | tf_op jit(solution)/shard_map/ppermute | solution.py:648
Sparse Core Ops, SparseCore 0:
  10.3 65.4 all-gather.3
